TPU v7x, 32 devices: a whole 2x2x4 slice. The times are simulated.
32 devices in a mesh: groups: 2 (over x), gx: 16 (over z, y, core).
Axes of the slice: x: 2, y: 2, z: 4, core: 2. Of those that a mesh axis runs over, the one named last changes fastest.
Arguments:
- u_prev: float32 [256, 256, 256], P(('groups', 'gx')), parts along dimension 0, may hold values from -7 to 7
- u_cur: float32 [256, 256, 256], P(('groups', 'gx')), parts along dimension 0, may hold values from -7 to 7
- courant_sq: float32 [256, 256, 256], P(('groups', 'gx')), parts along dimension 0, may hold values from 0.1 to 0.33
- patch_map: int32 [256, 4, 256], P(('groups', 'gx')), parts along dimension 0, may hold values from 0 to 159
- absorb: float32 [320], P('groups'), parts along dimension 0, may hold values from 0.05 to 1
- checkpoint: int32 [2], P('groups'), parts along dimension 0, may hold values from 0 to 60
- target_curve: float32 [128], P('groups'), parts along dimension 0, may hold values from 0 to 2.5
- tail_energy: float32 [2], P('groups'), parts along dimension 0, may hold values from 0.5 to 4
Outputs:
- grad_prev: float32 [256, 256, 256], P(('groups', 'gx')), parts along dimension 0
- grad_cur: float32 [256, 256, 256], P(('groups', 'gx')), parts along dimension 0
- grad_absorb: float32 [320], P(('groups', 'gx')), parts along dimension 0
There are 2 independent parts, one for each index of `groups`. A program takes and returns all parts, laid end to end along the dimension named above; each array names one. Nothing has to cross between parts.
All inputs are finite; a program needn't handle non-finite values.
Results may differ from a plain program's by a relative error of at most 0.00002.
Values sent between devices are 32-bit elements; how exact they have to be, the bound alone decides.
A program may use at most 128 MiB of HBM per device.

v0:
```python
import functools

import jax
import jax.numpy as jnp
from jax import lax
from jax.experimental import pallas as pl
from jax.experimental.pallas import tpu as pltpu
from jax.sharding import PartitionSpec as P

STEPS = 4
PATCH_CELLS = 819
PAD = 8
ROWS = 32
MESH = pl.DeviceIdType.MESH


def kernel(
    n, all_cells,
    prev_hbm, cur_hbm, courant_hbm, map_ref, absorb_ref, check_ref, target_ref, tail_ref,
    gprev_hbm, gcur_hbm, gabs_ref,
    u, p, last, prev, cs, damp, inv, w, gprev, gcur,
    map_t, faces, energy, emsg, eslots, gains, part, pslots,
    local_sem, send_sem, recv_sem, esend, erecv, psend, precv,
):
    me = lax.axis_index("gx")
    depth, side = prev.shape[0], prev.shape[1]
    chunks = side // ROWS
    patches = absorb_ref.shape[0]
    owned = patches // n
    inner = pl.ds(PAD, side)
    has_left, has_right = me > 0, me < n - 1

    loads = [
        pltpu.make_async_copy(cur_hbm, u.at[0, pl.ds(1, depth), inner, :], local_sem.at[0]),
        pltpu.make_async_copy(prev_hbm, prev, local_sem.at[1]),
        pltpu.make_async_copy(courant_hbm, cs, local_sem.at[2]),
    ]
    for copy in loads:
        copy.start()

    border = jnp.zeros((PAD, side), jnp.float32)
    for field in (u, p):
        for k in range(STEPS):
            def clear(x, carry, field=field, k=k):
                field[k, x, 0:PAD, :] = border
                field[k, x, PAD + side : PAD + side + PAD, :] = border
                return carry

            lax.fori_loop(0, depth + 2, clear, 0)

    def clear_halo(layer):
        for field in (u, p):
            for k in range(STEPS):
                field[k, layer, PAD : PAD + side, :] = jnp.zeros((side, side), jnp.float32)

    @pl.when(me == 0)
    def _():
        clear_halo(0)

    @pl.when(me == n - 1)
    def _():
        clear_halo(depth + 1)

    barrier = pltpu.get_barrier_semaphore()

    def greet(d, carry):
        pl.semaphore_signal(
            barrier, inc=1, device_id={"gx": lax.rem(me + d, n)}, device_id_type=MESH
        )
        return carry

    lax.fori_loop(1, n, greet, 0)
    pl.semaphore_wait(barrier, n - 1)

    def exchange(e):
        field, k = (u, e) if e < STEPS else (p, e - STEPS)
        low = cur_hbm.at[0] if e == 0 else field.at[k, 1, inner, :]
        high = cur_hbm.at[depth - 1] if e == 0 else field.at[k, depth, inner, :]
        to_left = pltpu.make_async_remote_copy(
            src_ref=low, dst_ref=field.at[k, depth + 1, inner, :],
            send_sem=send_sem.at[e, 0], recv_sem=recv_sem.at[e, 0],
            device_id={"gx": jnp.maximum(me - 1, 0)}, device_id_type=MESH,
        )
        to_right = pltpu.make_async_remote_copy(
            src_ref=high, dst_ref=field.at[k, 0, inner, :],
            send_sem=send_sem.at[e, 1], recv_sem=recv_sem.at[e, 1],
            device_id={"gx": jnp.minimum(me + 1, n - 1)}, device_id_type=MESH,
        )
        return to_left, to_right

    def send(e):
        to_left, to_right = exchange(e)
        pl.when(has_left)(to_left.start)
        pl.when(has_right)(to_right.start)

    def receive(e):
        to_left, to_right = exchange(e)
        pl.when(has_right)(to_left.wait_recv)
        pl.when(has_left)(to_right.wait_recv)

    def sent(e):
        to_left, to_right = exchange(e)
        pl.when(has_left)(to_left.wait_send)
        pl.when(has_right)(to_right.wait_send)

    send(0)

    lane = lax.broadcasted_iota(jnp.int32, (ROWS, side), 1)
    row = lax.broadcasted_iota(jnp.int32, (ROWS, side), 0)

    for x in range(depth):
        for f in range(4):
            map_t[f, x : x + 1, :] = map_ref[x, f : f + 1, :]
    maps = [map_t[f] for f in range(4)]

    def look_up(i, found):
        value = absorb_ref[i]
        return tuple(jnp.where(m == i, value, s) for m, s in zip(maps, found))

    found = lax.fori_loop(
        0, patches, look_up, tuple(jnp.zeros((depth, side), jnp.float32) for _ in range(4)),
        unroll=4,
    )
    for f in range(4):
        faces[f] = found[f]

    def spread(i, carry):
        x, r = i // chunks, (i % chunks) * ROWS
        r = pl.multiple_of(r, ROWS)
        at = row + r
        f0, f1, f2, f3 = (faces[f, pl.ds(x, 1), :] for f in range(4))
        diagonal = lane == at
        c2 = jnp.sum(jnp.where(diagonal, f2, 0.0), axis=1, keepdims=True)
        c3 = jnp.sum(jnp.where(diagonal, f3, 0.0), axis=1, keepdims=True)
        s = jnp.where(at == 0, f0, 0.0) + jnp.where(at == side - 1, f1, 0.0)
        s = s + jnp.where(lane == 0, c2, 0.0) + jnp.where(lane == side - 1, c3, 0.0)
        damp[x, pl.ds(r, ROWS), :] = s
        inv[x, pl.ds(r, ROWS), :] = 1.0 / (1.0 + s)
        return carry

    lax.fori_loop(0, depth * chunks, spread, 0)
    for copy in loads:
        copy.wait()

    def around(field, k, x, r):
        tall = field[k, x + 1, pl.ds(r, ROWS + 2 * PAD), :]
        mid = tall[PAD : PAD + ROWS]
        here = pl.ds(r + PAD, ROWS)
        total = field[k, x, here, :] + field[k, x + 2, here, :]
        total = total + tall[PAD - 1 : PAD - 1 + ROWS] + tall[PAD + 1 : PAD + 1 + ROWS]
        total = total + jnp.where(lane == 0, 0.0, pltpu.roll(mid, 1, 1))
        total = total + jnp.where(lane == side - 1, 0.0, pltpu.roll(mid, side - 1, 1))
        return mid, total

    def over(planes, body, init):
        ends = planes == "ends"
        count = 2 if ends else depth - 2

        def step(i, carry):
            layer = i // chunks
            x = layer * (depth - 1) if ends else layer + 1
            return body(x, pl.multiple_of((i % chunks) * ROWS, ROWS), carry)

        return lax.fori_loop(0, count * chunks, step, init)

    def forward(k):
        def body(x, r, acc):
            at = pl.ds(r, ROWS)
            here = pl.ds(r + PAD, ROWS)
            mid, total = around(u, k, x, r)
            prior = prev[x, at, :] if k == 0 else u[k - 1, x + 1, here, :]
            c = cs[x, at, :]
            scale = inv[x, at, :]
            new = (2.0 * mid - (1.0 - damp[x, at, :]) * prior + c * (total - 6.0 * mid)) * scale
            if k < STEPS - 1:
                u[k + 1, x + 1, here, :] = new
            else:
                last[x, at, :] = new
                weighted = scale * new
                w[STEPS - 1, x, at, :] = weighted
                p[0, x + 1, here, :] = c * weighted
            square = new * new
            for b in range(0, ROWS, 8):
                acc = acc + square[b : b + 8]
            return acc

        return body

    nothing = jnp.zeros((8, side), jnp.float32)
    for k in range(STEPS):
        receive(k)
        acc = over("ends", forward(k), nothing)
        send(k + 1)
        energy[k] = over("middle", forward(k), acc)

    emsg[...] = jnp.zeros_like(emsg)
    for k in range(STEPS):
        line = jnp.sum(energy[k], axis=0, keepdims=True)
        half = line[:, :128]
        for b in range(128, side, 128):
            half = half + line[:, b : b + 128]
        emsg[k : k + 1, :] = half

    def e_copy(d):
        return pltpu.make_async_remote_copy(
            src_ref=emsg, dst_ref=eslots.at[d], send_sem=esend.at[d], recv_sem=erecv.at[d],
            device_id={"gx": lax.rem(me + d, n)}, device_id_type=MESH,
        )

    def p_copy(d):
        to = lax.rem(me + d, n)
        return pltpu.make_async_remote_copy(
            src_ref=part.at[to], dst_ref=pslots.at[d], send_sem=psend.at[d], recv_sem=precv.at[d],
            device_id={"gx": to}, device_id_type=MESH,
        )

    def each(action):
        def step(d, carry):
            action(d)
            return carry

        lax.fori_loop(1, n, step, 0)

    each(lambda d: e_copy(d).start())
    each(lambda d: e_copy(d).wait_recv())
    summed = lax.fori_loop(1, n, lambda d, t: t + eslots[d], emsg[...])
    summed = jnp.sum(summed, axis=1, keepdims=True) / all_cells
    tail, start = tail_ref[0], check_ref[0]
    later = jnp.zeros((1, side), jnp.float32) + tail
    slopes = [None] * STEPS
    for k in range(STEPS - 1, -1, -1):
        later = later + summed[k : k + 1, :]
        slopes[k] = 2.0 * (jnp.log(later) - target_ref[start + k]) / later
    running = jnp.zeros((1, side), jnp.float32)
    for k in range(STEPS):
        running = running + slopes[k]
        gains[k : k + 1, :] = 2.0 * running

    def backward(j):
        slot = STEPS - j

        def body(x, r, carry):
            at = pl.ds(r, ROWS)
            here = pl.ds(r + PAD, ROWS)
            mid, total = around(p, slot, x, r)
            fresh = 2.0 * w[j - 1, x, at, :] + total - 6.0 * mid
            if j == STEPS:
                fresh = fresh * gains[STEPS - 1 : STEPS, :]
            else:
                after = w[j, x, at, :]
                if j == STEPS - 1:
                    after = after * gains[STEPS - 1 : STEPS, :]
                fresh = fresh - (1.0 - damp[x, at, :]) * after
            if j == 1:
                gcur[x, at, :] = fresh
                return carry
            fresh = fresh + gains[j - 2 : j - 1, :] * u[j - 1, x + 1, here, :]
            weighted = inv[x, at, :] * fresh
            w[j - 2, x, at, :] = weighted
            p[slot + 1, x + 1, here, :] = cs[x, at, :] * weighted
            if j == 2:
                gprev[x, at, :] = (damp[x, at, :] - 1.0) * weighted
            return carry

        return body

    for j in range(STEPS, 1, -1):
        receive(2 * STEPS - j)
        over("ends", backward(j), 0)
        send(2 * STEPS - j + 1)
        over("middle", backward(j), 0)

    out_prev = pltpu.make_async_copy(gprev, gprev_hbm, local_sem.at[3])
    out_prev.start()

    def state(k, x, at, cells):
        if k < 0:
            return prev[x, at, cells]
        if k == STEPS:
            return last[x, at, cells]
        return u[k, x + 1, pl.ds(at.start + PAD, at.size), cells]

    def product(x, at, cells):
        total = None
        for j in range(STEPS, 0, -1):
            term = w[j - 1, x, at, cells] * (state(j - 2, x, at, cells) - state(j, x, at, cells))
            if j == STEPS:
                term = term * gains[STEPS - 1 : STEPS, cells]
            total = term if total is None else total + term
        return total

    def collect(x, carry):
        top = product(x, pl.ds(0, 8), slice(0, side))
        bottom = product(x, pl.ds(side - 8, 8), slice(0, side))
        faces[0, pl.ds(x, 1), :] = top[0:1]
        faces[1, pl.ds(x, 1), :] = bottom[7:8]

        def column(i, lines):
            r = pl.multiple_of(i * ROWS, ROWS)
            diagonal = lane == row + r
            at = pl.ds(r, ROWS)
            left = product(x, at, slice(0, 128))[:, 0:1]
            right = product(x, at, slice(side - 128, side))[:, 127:128]
            return tuple(
                line + jnp.sum(jnp.where(diagonal, c, 0.0), axis=0, keepdims=True)
                for line, c in zip(lines, (left, right))
            )

        blank = jnp.zeros((1, side), jnp.float32)
        lines = lax.fori_loop(0, chunks, column, (blank, blank))
        faces[2, pl.ds(x, 1), :] = lines[0]
        faces[3, pl.ds(x, 1), :] = lines[1]
        return carry

    lax.fori_loop(0, depth, collect, 0)
    place = lax.broadcasted_iota(jnp.int32, (8, 128), 1)

    def by_owner(i, carry):
        tile = jnp.zeros((8, 128), jnp.float32)
        for k in range(owned):
            hit = None
            for f in range(4):
                term = jnp.where(map_t[f] == i * owned + k, faces[f], 0.0)
                hit = term if hit is None else hit + term
            line = jnp.sum(hit, axis=0, keepdims=True)
            whole = jnp.sum(line, axis=1, keepdims=True)
            tile = jnp.where(place == k, whole, tile)
        part[i] = tile
        return carry

    lax.fori_loop(0, n, by_owner, 0)
    each(lambda d: p_copy(d).start())

    over("middle", backward(1), 0)
    ends = depth - 2
    out_mid = pltpu.make_async_copy(
        gcur.at[pl.ds(1, ends)], gcur_hbm.at[pl.ds(1, ends)], local_sem.at[4]
    )
    out_mid.start()
    receive(2 * STEPS - 1)
    over("ends", backward(1), 0)
    out_low = pltpu.make_async_copy(gcur.at[0], gcur_hbm.at[0], local_sem.at[5])
    out_high = pltpu.make_async_copy(gcur.at[depth - 1], gcur_hbm.at[depth - 1], local_sem.at[6])
    out_low.start()
    out_high.start()

    each(lambda d: p_copy(d).wait_recv())
    mine = lax.fori_loop(1, n, lambda d, t: t + pslots[d], part[me])
    gabs_ref[...] = mine / float(PATCH_CELLS)

    for e in range(2 * STEPS):
        sent(e)
    each(lambda d: e_copy(d).wait_send())
    each(lambda d: p_copy(d).wait_send())
    for copy in (out_prev, out_mid, out_low, out_high):
        copy.wait()


def on_device(n, u_prev, u_cur, courant_sq, patch_map, absorb, checkpoint, target_curve, tail_energy):
    depth, side = u_cur.shape[0], u_cur.shape[1]
    f32 = jnp.float32
    brick = pltpu.VMEM((depth, side, side), f32)
    padded = pltpu.VMEM((STEPS, depth + 2, side + 2 * PAD, side), f32)
    hbm = pl.BlockSpec(memory_space=pl.ANY)
    vmem = pl.BlockSpec(memory_space=pltpu.VMEM)
    smem = pl.BlockSpec(memory_space=pltpu.SMEM)
    dma = pltpu.SemaphoreType.DMA
    grad_prev, grad_cur, tile = pl.pallas_call(
        functools.partial(kernel, n, float(depth * n * side * side)),
        out_shape=(
            jax.ShapeDtypeStruct(u_cur.shape, f32),
            jax.ShapeDtypeStruct(u_cur.shape, f32),
            jax.ShapeDtypeStruct((8, 128), f32),
        ),
        in_specs=[hbm, hbm, hbm, vmem, smem, smem, smem, smem],
        out_specs=(hbm, hbm, vmem),
        scratch_shapes=[
            padded, padded, brick, brick, brick, brick, brick,
            pltpu.VMEM((STEPS, depth, side, side), f32), brick, brick,
            pltpu.VMEM((4, depth, side), jnp.int32),
            pltpu.VMEM((4, depth, side), f32),
            pltpu.VMEM((STEPS, 8, side), f32),
            pltpu.VMEM((8, 128), f32),
            pltpu.VMEM((n, 8, 128), f32),
            pltpu.VMEM((8, side), f32),
            pltpu.VMEM((n, 8, 128), f32),
            pltpu.VMEM((n, 8, 128), f32),
            dma((7,)), dma((2 * STEPS, 2)), dma((2 * STEPS, 2)),
            dma((n,)), dma((n,)), dma((n,)), dma((n,)),
        ],
        compiler_params=pltpu.CompilerParams(
            collective_id=0, has_side_effects=True, vmem_limit_bytes=56 * 1024 * 1024
        ),
    )(u_prev, u_cur, courant_sq, patch_map, absorb, checkpoint, target_curve, tail_energy)
    return grad_prev, grad_cur, tile[0, : absorb.shape[0] // n]


def solution(mesh):
    field = P(("groups", "gx"), None, None)
    return jax.shard_map(
        functools.partial(on_device, mesh.shape["gx"]),
        mesh=mesh,
        in_specs=(field, field, field, field, P("groups"), P("groups"), P("groups"), P("groups")),
        out_specs=(field, field, P(("groups", "gx"))),
        check_vma=False,
    )
```

profile of v0, /device:TPU:0, one launch (start us, length us, event | category | flops | bytes accessed | tf_op | source)
XLA Modules:
  0.0 94.0 jit_solution(10529762848949889738)
XLA Ops:
  1.9 86.3 %shard_map.103 = (f32[8,256,256]{2,1,0:T(8,128)}, f32[8,256,256]{2,1,0:T(8,128)}, f32[8,128]{1,0:T(8,128)}) custom-call(f32[8,256,256]{2,1,0:T(8,128)} %prev_hbm.1, f32[8,256,256]{2,1,0:T(8,128)} %cur_hbm.1, f32[8,256,256]{2,1,0:T(8,128)} %courant_hbm.1, s32[8,4,256]{2,1,0:T(4,128)} %map_ref.1, f32[160]{0:T(256)} %absorb_ref.1, s32[1]{0:T(128)S(6)} %copy.13.check_ref, ...), custom_call_target="tpu_custom_call" | custom-call | tf_op jit(solution)/shard_map/pallas_call | solution.py:368
  88.2 1.2 %slice_bitcast_fusion = f32[10]{0:T(128)} fusion(f32[8,128]{1,0:T(8,128)} %get-tuple-element.8), kind=kLoop, calls=%fused_computation | loop fusion | bytes 80 | tf_op jit(solution)/shard_map/squeeze | solution.py:395
  89.4 0.0 copy-start
  89.4 3.2 %copy.15 = f32[8,256,256]{2,1,0:T(8,128)} copy(f32[8,256,256]{2,1,0:T(8,128)} %get-tuple-element.12) | data formatting | bytes 4194304
  92.6 0.0 copy-done
  92.6 1.3 %copy.16 = f32[8,256,256]{2,1,0:T(8,128)} copy(f32[8,256,256]{2,1,0:T(8,128)S(1)} %copy-done) | data formatting | bytes 4194304
Async XLA Ops:
  89.4 3.2 %copy-start = (f32[8,256,256]{2,1,0:T(8,128)S(1)}, f32[8,256,256]{2,1,0:T(8,128)}, u32[]{:S(2)}) copy-start(f32[8,256,256]{2,1,0:T(8,128)} %get-tuple-element.13) | copy-start | bytes 6291460
where the time goes:
time: 95 us; the launch traced here: 94 us
  Pallas kernels  86.3 us (91%)
  local copies, waits for them, and re-layouts  5.7 us (6%)
  between operations  1.93 us (2%)
    pallas_call x1, Pallas kernels, on_device(): pl.pallas_call(functools.partial(kernel, n, float(depth * n * side * side...  86.3 us
    unnamed x4, local copies, waits for them, and re-layouts  4.52 us

commit v1 on v0

--- a/solution.py
+++ b/solution.py
@@ -11,6 +11,7 @@
 PATCH_CELLS = 819
 PAD = 8
 ROWS = 32
+BLOCKS = 2
 MESH = pl.DeviceIdType.MESH
 
 
@@ -24,7 +25,6 @@
 ):
     me = lax.axis_index("gx")
     depth, side = prev.shape[0], prev.shape[1]
-    chunks = side // ROWS
     patches = absorb_ref.shape[0]
     owned = patches // n
     inner = pl.ds(PAD, side)
@@ -72,38 +72,43 @@
     lax.fori_loop(1, n, greet, 0)
     pl.semaphore_wait(barrier, n - 1)
 
-    def exchange(e):
+    span = side // BLOCKS
+
+    def exchange(e, to_right, b):
         field, k = (u, e) if e < STEPS else (p, e - STEPS)
-        low = cur_hbm.at[0] if e == 0 else field.at[k, 1, inner, :]
-        high = cur_hbm.at[depth - 1] if e == 0 else field.at[k, depth, inner, :]
-        to_left = pltpu.make_async_remote_copy(
-            src_ref=low, dst_ref=field.at[k, depth + 1, inner, :],
-            send_sem=send_sem.at[e, 0], recv_sem=recv_sem.at[e, 0],
-            device_id={"gx": jnp.maximum(me - 1, 0)}, device_id_type=MESH,
+        rows = pl.ds(PAD + b * span, span)
+        layer, landing = (depth, 0) if to_right else (1, depth + 1)
+        way = 1 if to_right else 0
+        to = jnp.minimum(me + 1, n - 1) if to_right else jnp.maximum(me - 1, 0)
+        source = field.at[k, layer, rows, :]
+        if e == 0:
+            source = cur_hbm.at[layer - 1, pl.ds(b * span, span), :]
+        return pltpu.make_async_remote_copy(
+            src_ref=source, dst_ref=field.at[k, landing, rows, :],
+            send_sem=send_sem.at[e, way, b], recv_sem=recv_sem.at[e, way, b],
+            device_id={"gx": to}, device_id_type=MESH,
         )
-        to_right = pltpu.make_async_remote_copy(
-            src_ref=high, dst_ref=field.at[k, 0, inner, :],
-            send_sem=send_sem.at[e, 1], recv_sem=recv_sem.at[e, 1],
-            device_id={"gx": jnp.minimum(me + 1, n - 1)}, device_id_type=MESH,
-        )
-        return to_left, to_right
-
-    def send(e):
-        to_left, to_right = exchange(e)
-        pl.when(has_left)(to_left.start)
-        pl.when(has_right)(to_right.start)
-
-    def receive(e):
-        to_left, to_right = exchange(e)
-        pl.when(has_right)(to_left.wait_recv)
-        pl.when(has_left)(to_right.wait_recv)
+
+    def send(e, to_right, b):
+        @pl.when(has_right if to_right else has_left)
+        def _():
+            exchange(e, to_right, b).start()
+
+    def receive(e, from_left, b):
+        @pl.when(has_left if from_left else has_right)
+        def _():
+            exchange(e, from_left, b).wait_recv()
 
     def sent(e):
-        to_left, to_right = exchange(e)
-        pl.when(has_left)(to_left.wait_send)
-        pl.when(has_right)(to_right.wait_send)
-
-    send(0)
+        for to_right, there in ((False, has_left), (True, has_right)):
+            @pl.when(there)
+            def _(to_right=to_right):
+                for b in range(BLOCKS):
+                    exchange(e, to_right, b).wait_send()
+
+    for b in range(BLOCKS):
+        send(0, False, b)
+        send(0, True, b)
 
     lane = lax.broadcasted_iota(jnp.int32, (ROWS, side), 1)
     row = lax.broadcasted_iota(jnp.int32, (ROWS, side), 0)
@@ -124,21 +129,22 @@
     for f in range(4):
         faces[f] = found[f]
 
-    def spread(i, carry):
-        x, r = i // chunks, (i % chunks) * ROWS
-        r = pl.multiple_of(r, ROWS)
-        at = row + r
+    def spread(x, carry):
         f0, f1, f2, f3 = (faces[f, pl.ds(x, 1), :] for f in range(4))
-        diagonal = lane == at
-        c2 = jnp.sum(jnp.where(diagonal, f2, 0.0), axis=1, keepdims=True)
-        c3 = jnp.sum(jnp.where(diagonal, f3, 0.0), axis=1, keepdims=True)
-        s = jnp.where(at == 0, f0, 0.0) + jnp.where(at == side - 1, f1, 0.0)
-        s = s + jnp.where(lane == 0, c2, 0.0) + jnp.where(lane == side - 1, c3, 0.0)
-        damp[x, pl.ds(r, ROWS), :] = s
-        inv[x, pl.ds(r, ROWS), :] = 1.0 / (1.0 + s)
+        for r in range(0, side, ROWS):
+            diagonal = lane == row + r
+            c2 = jnp.sum(jnp.where(diagonal, f2, 0.0), axis=1, keepdims=True)
+            c3 = jnp.sum(jnp.where(diagonal, f3, 0.0), axis=1, keepdims=True)
+            s = jnp.where(lane == 0, c2, 0.0) + jnp.where(lane == side - 1, c3, 0.0)
+            if r == 0:
+                s = s + jnp.where(row == 0, f0, 0.0)
+            if r == side - ROWS:
+                s = s + jnp.where(row == ROWS - 1, f1, 0.0)
+            damp[x, r : r + ROWS, :] = s
+            inv[x, r : r + ROWS, :] = 1.0 / (1.0 + s)
         return carry
 
-    lax.fori_loop(0, depth * chunks, spread, 0)
+    lax.fori_loop(0, depth, spread, 0)
     for copy in loads:
         copy.wait()
 
@@ -152,16 +158,23 @@
         total = total + jnp.where(lane == side - 1, 0.0, pltpu.roll(mid, side - 1, 1))
         return mid, total
 
-    def over(planes, body, init):
-        ends = planes == "ends"
-        count = 2 if ends else depth - 2
-
-        def step(i, carry):
-            layer = i // chunks
-            x = layer * (depth - 1) if ends else layer + 1
-            return body(x, pl.multiple_of((i % chunks) * ROWS, ROWS), carry)
-
-        return lax.fori_loop(0, count * chunks, step, init)
+    def middle(body, carry):
+        def step(x, carry):
+            for r in range(0, side, ROWS):
+                carry = body(x, r, carry)
+            return carry
+
+        return lax.fori_loop(1, depth - 1, step, carry)
+
+    def outer(e, body, carry, last_one=False):
+        for b in range(BLOCKS):
+            for x, is_right in ((0, False), (depth - 1, True)):
+                receive(e, not is_right, b)
+                for r in range(b * span, (b + 1) * span, ROWS):
+                    carry = body(x, r, carry)
+                if not last_one:
+                    send(e + 1, is_right, b)
+        return carry
 
     def forward(k):
         def body(x, r, acc):
@@ -188,10 +201,8 @@
 
     nothing = jnp.zeros((8, side), jnp.float32)
     for k in range(STEPS):
-        receive(k)
-        acc = over("ends", forward(k), nothing)
-        send(k + 1)
-        energy[k] = over("middle", forward(k), acc)
+        acc = outer(k, forward(k), nothing)
+        energy[k] = middle(forward(k), acc)
 
     emsg[...] = jnp.zeros_like(emsg)
     for k in range(STEPS):
@@ -265,10 +276,8 @@
         return body
 
     for j in range(STEPS, 1, -1):
-        receive(2 * STEPS - j)
-        over("ends", backward(j), 0)
-        send(2 * STEPS - j + 1)
-        over("middle", backward(j), 0)
+        outer(2 * STEPS - j, backward(j), 0)
+        middle(backward(j), 0)
 
     out_prev = pltpu.make_async_copy(gprev, gprev_hbm, local_sem.at[3])
     out_prev.start()
@@ -295,32 +304,31 @@
         faces[0, pl.ds(x, 1), :] = top[0:1]
         faces[1, pl.ds(x, 1), :] = bottom[7:8]
 
-        def column(i, lines):
-            r = pl.multiple_of(i * ROWS, ROWS)
+        lines = [jnp.zeros((1, side), jnp.float32)] * 2
+        for r in range(0, side, ROWS):
             diagonal = lane == row + r
             at = pl.ds(r, ROWS)
             left = product(x, at, slice(0, 128))[:, 0:1]
             right = product(x, at, slice(side - 128, side))[:, 127:128]
-            return tuple(
+            lines = [
                 line + jnp.sum(jnp.where(diagonal, c, 0.0), axis=0, keepdims=True)
                 for line, c in zip(lines, (left, right))
-            )
-
-        blank = jnp.zeros((1, side), jnp.float32)
-        lines = lax.fori_loop(0, chunks, column, (blank, blank))
+            ]
         faces[2, pl.ds(x, 1), :] = lines[0]
         faces[3, pl.ds(x, 1), :] = lines[1]
         return carry
 
     lax.fori_loop(0, depth, collect, 0)
     place = lax.broadcasted_iota(jnp.int32, (8, 128), 1)
+
+    walls = [faces[f] for f in range(4)]
 
     def by_owner(i, carry):
         tile = jnp.zeros((8, 128), jnp.float32)
         for k in range(owned):
             hit = None
             for f in range(4):
-                term = jnp.where(map_t[f] == i * owned + k, faces[f], 0.0)
+                term = jnp.where(maps[f] == i * owned + k, walls[f], 0.0)
                 hit = term if hit is None else hit + term
             line = jnp.sum(hit, axis=0, keepdims=True)
             whole = jnp.sum(line, axis=1, keepdims=True)
@@ -331,14 +339,13 @@
     lax.fori_loop(0, n, by_owner, 0)
     each(lambda d: p_copy(d).start())
 
-    over("middle", backward(1), 0)
+    middle(backward(1), 0)
     ends = depth - 2
     out_mid = pltpu.make_async_copy(
         gcur.at[pl.ds(1, ends)], gcur_hbm.at[pl.ds(1, ends)], local_sem.at[4]
     )
     out_mid.start()
-    receive(2 * STEPS - 1)
-    over("ends", backward(1), 0)
+    outer(2 * STEPS - 1, backward(1), 0, last_one=True)
     out_low = pltpu.make_async_copy(gcur.at[0], gcur_hbm.at[0], local_sem.at[5])
     out_high = pltpu.make_async_copy(gcur.at[depth - 1], gcur_hbm.at[depth - 1], local_sem.at[6])
     out_low.start()
@@ -385,7 +392,7 @@
             pltpu.VMEM((8, side), f32),
             pltpu.VMEM((n, 8, 128), f32),
             pltpu.VMEM((n, 8, 128), f32),
-            dma((7,)), dma((2 * STEPS, 2)), dma((2 * STEPS, 2)),
+            dma((7,)), dma((2 * STEPS, 2, BLOCKS)), dma((2 * STEPS, 2, BLOCKS)),
             dma((n,)), dma((n,)), dma((n,)), dma((n,)),
         ],
         compiler_params=pltpu.CompilerParams(

time: 95 us -> 77 us (0.81)
  Pallas kernels: 86.3 us -> 69.1 us
    pallas_call x1, Pallas kernels: 86.3 us -> 69.1 us  [on_device(): pl.pallas_call(functools.partial(kernel, n, float(depth * n * side * side...]
where the time goes in v1:
time: 77 us; the launch traced here: 76.7 us
  Pallas kernels  69.1 us (90%)
  local copies, waits for them, and re-layouts  5.7 us (7%)
  between operations  1.93 us (3%)
    pallas_call x1, Pallas kernels, on_device(): pl.pallas_call(functools.partial(kernel, n, float(depth * n * side * side...  69.1 us
    unnamed x4, local copies, waits for them, and re-layouts  4.52 us

profile of v1, /device:TPU:0, one launch (start us, length us, event | category | flops | bytes accessed | tf_op | source)
XLA Modules:
  0.0 76.7 jit_solution(3649543139876378261)
XLA Ops:
  1.9 69.1 %shard_map.103 = (f32[8,256,256]{2,1,0:T(8,128)}, f32[8,256,256]{2,1,0:T(8,128)}, f32[8,128]{1,0:T(8,128)}) custom-call(f32[8,256,256]{2,1,0:T(8,128)} %prev_hbm.1, f32[8,256,256]{2,1,0:T(8,128)} %cur_hbm.1, f32[8,256,256]{2,1,0:T(8,128)} %courant_hbm.1, s32[8,4,256]{2,1,0:T(4,128)} %map_ref.1, f32[160]{0:T(256)} %absorb_ref.1, s32[1]{0:T(128)S(6)} %copy.13.check_ref, ...), custom_call_target="tpu_custom_call" | custom-call | tf_op jit(solution)/shard_map/pallas_call | solution.py:375
  71.0 1.2 %slice_bitcast_fusion = f32[10]{0:T(128)} fusion(f32[8,128]{1,0:T(8,128)} %get-tuple-element.8), kind=kLoop, calls=%fused_computation | loop fusion | bytes 80 | tf_op jit(solution)/shard_map/squeeze | solution.py:402
  72.2 0.0 copy-start
  72.2 3.2 %copy.15 = f32[8,256,256]{2,1,0:T(8,128)} copy(f32[8,256,256]{2,1,0:T(8,128)} %get-tuple-element.12) | data formatting | bytes 4194304
  75.4 0.0 copy-done
  75.4 1.3 %copy.16 = f32[8,256,256]{2,1,0:T(8,128)} copy(f32[8,256,256]{2,1,0:T(8,128)S(1)} %copy-done) | data formatting | bytes 4194304
Async XLA Ops:
  72.2 3.2 %copy-start = (f32[8,256,256]{2,1,0:T(8,128)S(1)}, f32[8,256,256]{2,1,0:T(8,128)}, u32[]{:S(2)}) copy-start(f32[8,256,256]{2,1,0:T(8,128)} %get-tuple-element.13) | copy-start | bytes 6291460

commit v2 on v1

--- a/solution.py
+++ b/solution.py
@@ -18,8 +18,8 @@
 def kernel(
     n, all_cells,
     prev_hbm, cur_hbm, courant_hbm, map_ref, absorb_ref, check_ref, target_ref, tail_ref,
-    gprev_hbm, gcur_hbm, gabs_ref,
-    u, p, last, prev, cs, damp, inv, w, gprev, gcur,
+    gprev, gcur, gabs_ref,
+    u, p, last, prev, cs, damp, inv, w,
     map_t, faces, energy, emsg, eslots, gains, part, pslots,
     local_sem, send_sem, recv_sem, esend, erecv, psend, precv,
 ):
@@ -37,29 +37,6 @@
     ]
     for copy in loads:
         copy.start()
-
-    border = jnp.zeros((PAD, side), jnp.float32)
-    for field in (u, p):
-        for k in range(STEPS):
-            def clear(x, carry, field=field, k=k):
-                field[k, x, 0:PAD, :] = border
-                field[k, x, PAD + side : PAD + side + PAD, :] = border
-                return carry
-
-            lax.fori_loop(0, depth + 2, clear, 0)
-
-    def clear_halo(layer):
-        for field in (u, p):
-            for k in range(STEPS):
-                field[k, layer, PAD : PAD + side, :] = jnp.zeros((side, side), jnp.float32)
-
-    @pl.when(me == 0)
-    def _():
-        clear_halo(0)
-
-    @pl.when(me == n - 1)
-    def _():
-        clear_halo(depth + 1)
 
     barrier = pltpu.get_barrier_semaphore()
 
@@ -109,6 +86,29 @@
     for b in range(BLOCKS):
         send(0, False, b)
         send(0, True, b)
+
+    border = jnp.zeros((PAD, side), jnp.float32)
+    for field in (u, p):
+        for k in range(STEPS):
+            def clear(x, carry, field=field, k=k):
+                field[k, x, 0:PAD, :] = border
+                field[k, x, PAD + side : PAD + side + PAD, :] = border
+                return carry
+
+            lax.fori_loop(0, depth + 2, clear, 0)
+
+    def clear_halo(layer):
+        for field in (u, p):
+            for k in range(STEPS):
+                field[k, layer, PAD : PAD + side, :] = jnp.zeros((side, side), jnp.float32)
+
+    @pl.when(me == 0)
+    def _():
+        clear_halo(0)
+
+    @pl.when(me == n - 1)
+    def _():
+        clear_halo(depth + 1)
 
     lane = lax.broadcasted_iota(jnp.int32, (ROWS, side), 1)
     row = lax.broadcasted_iota(jnp.int32, (ROWS, side), 0)
@@ -275,13 +275,6 @@
 
         return body
 
-    for j in range(STEPS, 1, -1):
-        outer(2 * STEPS - j, backward(j), 0)
-        middle(backward(j), 0)
-
-    out_prev = pltpu.make_async_copy(gprev, gprev_hbm, local_sem.at[3])
-    out_prev.start()
-
     def state(k, x, at, cells):
         if k < 0:
             return prev[x, at, cells]
@@ -289,36 +282,47 @@
             return last[x, at, cells]
         return u[k, x + 1, pl.ds(at.start + PAD, at.size), cells]
 
-    def product(x, at, cells):
+    def product(steps, x, at, cells):
         total = None
-        for j in range(STEPS, 0, -1):
+        for j in steps:
             term = w[j - 1, x, at, cells] * (state(j - 2, x, at, cells) - state(j, x, at, cells))
             if j == STEPS:
                 term = term * gains[STEPS - 1 : STEPS, cells]
             total = term if total is None else total + term
         return total
 
-    def collect(x, carry):
-        top = product(x, pl.ds(0, 8), slice(0, side))
-        bottom = product(x, pl.ds(side - 8, 8), slice(0, side))
-        faces[0, pl.ds(x, 1), :] = top[0:1]
-        faces[1, pl.ds(x, 1), :] = bottom[7:8]
+    def collect(steps, x, carry):
+        first = STEPS in steps
+
+        def keep(f, line):
+            faces[f, pl.ds(x, 1), :] = line if first else faces[f, pl.ds(x, 1), :] + line
+
+        top = product(steps, x, pl.ds(0, 8), slice(0, side))
+        bottom = product(steps, x, pl.ds(side - 8, 8), slice(0, side))
+        keep(0, top[0:1])
+        keep(1, bottom[7:8])
 
         lines = [jnp.zeros((1, side), jnp.float32)] * 2
         for r in range(0, side, ROWS):
             diagonal = lane == row + r
             at = pl.ds(r, ROWS)
-            left = product(x, at, slice(0, 128))[:, 0:1]
-            right = product(x, at, slice(side - 128, side))[:, 127:128]
+            left = product(steps, x, at, slice(0, 128))[:, 0:1]
+            right = product(steps, x, at, slice(side - 128, side))[:, 127:128]
             lines = [
                 line + jnp.sum(jnp.where(diagonal, c, 0.0), axis=0, keepdims=True)
                 for line, c in zip(lines, (left, right))
             ]
-        faces[2, pl.ds(x, 1), :] = lines[0]
-        faces[3, pl.ds(x, 1), :] = lines[1]
+        keep(2, lines[0])
+        keep(3, lines[1])
         return carry
 
-    lax.fori_loop(0, depth, collect, 0)
+    for j in range(STEPS, 1, -1):
+        outer(2 * STEPS - j, backward(j), 0)
+        middle(backward(j), 0)
+        if j == 3:
+            lax.fori_loop(0, depth, functools.partial(collect, (4, 3, 2)), 0)
+    lax.fori_loop(0, depth, functools.partial(collect, (1,)), 0)
+
     place = lax.broadcasted_iota(jnp.int32, (8, 128), 1)
 
     walls = [faces[f] for f in range(4)]
@@ -340,16 +344,7 @@
     each(lambda d: p_copy(d).start())
 
     middle(backward(1), 0)
-    ends = depth - 2
-    out_mid = pltpu.make_async_copy(
-        gcur.at[pl.ds(1, ends)], gcur_hbm.at[pl.ds(1, ends)], local_sem.at[4]
-    )
-    out_mid.start()
     outer(2 * STEPS - 1, backward(1), 0, last_one=True)
-    out_low = pltpu.make_async_copy(gcur.at[0], gcur_hbm.at[0], local_sem.at[5])
-    out_high = pltpu.make_async_copy(gcur.at[depth - 1], gcur_hbm.at[depth - 1], local_sem.at[6])
-    out_low.start()
-    out_high.start()
 
     each(lambda d: p_copy(d).wait_recv())
     mine = lax.fori_loop(1, n, lambda d, t: t + pslots[d], part[me])
@@ -359,8 +354,6 @@
         sent(e)
     each(lambda d: e_copy(d).wait_send())
     each(lambda d: p_copy(d).wait_send())
-    for copy in (out_prev, out_mid, out_low, out_high):
-        copy.wait()
 
 
 def on_device(n, u_prev, u_cur, courant_sq, patch_map, absorb, checkpoint, target_curve, tail_energy):
@@ -375,15 +368,15 @@
     grad_prev, grad_cur, tile = pl.pallas_call(
         functools.partial(kernel, n, float(depth * n * side * side)),
         out_shape=(
-            jax.ShapeDtypeStruct(u_cur.shape, f32),
-            jax.ShapeDtypeStruct(u_cur.shape, f32),
+            pltpu.VMEM(u_cur.shape, f32),
+            pltpu.VMEM(u_cur.shape, f32),
             jax.ShapeDtypeStruct((8, 128), f32),
         ),
         in_specs=[hbm, hbm, hbm, vmem, smem, smem, smem, smem],
-        out_specs=(hbm, hbm, vmem),
+        out_specs=(vmem, vmem, vmem),
         scratch_shapes=[
             padded, padded, brick, brick, brick, brick, brick,
-            pltpu.VMEM((STEPS, depth, side, side), f32), brick, brick,
+            pltpu.VMEM((STEPS, depth, side, side), f32),
             pltpu.VMEM((4, depth, side), jnp.int32),
             pltpu.VMEM((4, depth, side), f32),
             pltpu.VMEM((STEPS, 8, side), f32),

time: 77 us -> 74.4 us (0.966)
  local copies, waits for them, and re-layouts: 5.7 us -> 3.82 us
    unnamed x4 -> x2, local copies, waits for them, and re-layouts: 4.52 us -> 2.64 us
where the time goes in v2:
time: 74.4 us; the launch traced here: 74.2 us
  Pallas kernels  68.4 us (92%)
  local copies, waits for them, and re-layouts  3.82 us (5%)
  between operations  1.93 us (3%)
    pallas_call x1, Pallas kernels, on_device(): pl.pallas_call(functools.partial(kernel, n, float(depth * n * side * side...  68.4 us
    unnamed x2, local copies, waits for them, and re-layouts  2.64 us

profile of v2, /device:TPU:0, one launch (start us, length us, event | category | flops | bytes accessed | tf_op | source)
XLA Modules:
  0.0 74.2 jit_solution(889987346385516109)
XLA Ops:
  1.9 68.4 %shard_map.103 = (f32[8,256,256]{2,1,0:T(8,128)S(1)}, f32[8,256,256]{2,1,0:T(8,128)S(1)}, f32[8,128]{1,0:T(8,128)}) custom-call(f32[8,256,256]{2,1,0:T(8,128)} %prev_hbm.1, f32[8,256,256]{2,1,0:T(8,128)} %cur_hbm.1, f32[8,256,256]{2,1,0:T(8,128)} %courant_hbm.1, s32[8,4,256]{2,1,0:T(4,128)} %map_ref.1, f32[160]{0:T(256)} %absorb_ref.1, ...), custom_call_target="tpu_custom_call" | custom-call | tf_op jit(solution)/shard_map/pallas_call | solution.py:368
  70.4 1.3 %copy.13 = f32[8,256,256]{2,1,0:T(8,128)} copy(f32[8,256,256]{2,1,0:T(8,128)S(1)} %get-tuple-element.9) | data formatting | bytes 4194304
  71.7 1.2 %slice_bitcast_fusion = f32[10]{0:T(128)} fusion(f32[8,128]{1,0:T(8,128)} %get-tuple-element.8), kind=kLoop, calls=%fused_computation | loop fusion | bytes 80 | tf_op jit(solution)/shard_map/squeeze | solution.py:395
  72.9 1.3 %copy.14 = f32[8,256,256]{2,1,0:T(8,128)} copy(f32[8,256,256]{2,1,0:T(8,128)S(1)} %get-tuple-element.10) | data formatting | bytes 4194304

commit v3 on v2

--- a/solution.py
+++ b/solution.py
@@ -201,8 +201,10 @@
 
     nothing = jnp.zeros((8, side), jnp.float32)
     for k in range(STEPS):
-        acc = outer(k, forward(k), nothing)
-        energy[k] = middle(forward(k), acc)
+        if k == STEPS - 1:
+            energy[k] = outer(k, forward(k), middle(forward(k), nothing))
+        else:
+            energy[k] = middle(forward(k), outer(k, forward(k), nothing))
 
     emsg[...] = jnp.zeros_like(emsg)
     for k in range(STEPS):

time: 74.4 us -> 74.3 us (level)
  no operation moved by 1% of the time
where the time goes in v3:
time: 74.3 us; the launch traced here: 74.1 us
  Pallas kernels  68.4 us (92%)
  local copies, waits for them, and re-layouts  3.82 us (5%)
  between operations  1.93 us (3%)
    pallas_call x1, Pallas kernels, on_device(): pl.pallas_call(functools.partial(kernel, n, float(depth * n * side * side...  68.4 us
    unnamed x2, local copies, waits for them, and re-layouts  2.64 us

profile of v3, /device:TPU:0, one launch (start us, length us, event | category | flops | bytes accessed | tf_op | source)
XLA Modules:
  0.0 74.1 jit_solution(17970040380566895623)
XLA Ops:
  1.9 68.4 %shard_map.103 = (f32[8,256,256]{2,1,0:T(8,128)S(1)}, f32[8,256,256]{2,1,0:T(8,128)S(1)}, f32[8,128]{1,0:T(8,128)}) custom-call(f32[8,256,256]{2,1,0:T(8,128)} %prev_hbm.1, f32[8,256,256]{2,1,0:T(8,128)} %cur_hbm.1, f32[8,256,256]{2,1,0:T(8,128)} %courant_hbm.1, s32[8,4,256]{2,1,0:T(4,128)} %map_ref.1, f32[160]{0:T(256)} %absorb_ref.1, ...), custom_call_target="tpu_custom_call" | custom-call | tf_op jit(solution)/shard_map/pallas_call | solution.py:370
  70.3 1.3 %copy.13 = f32[8,256,256]{2,1,0:T(8,128)} copy(f32[8,256,256]{2,1,0:T(8,128)S(1)} %get-tuple-element.9) | data formatting | bytes 4194304
  71.6 1.2 %slice_bitcast_fusion = f32[10]{0:T(128)} fusion(f32[8,128]{1,0:T(8,128)} %get-tuple-element.8), kind=kLoop, calls=%fused_computation | loop fusion | bytes 80 | tf_op jit(solution)/shard_map/squeeze | solution.py:397
  72.8 1.3 %copy.14 = f32[8,256,256]{2,1,0:T(8,128)} copy(f32[8,256,256]{2,1,0:T(8,128)S(1)} %get-tuple-element.10) | data formatting | bytes 4194304
